TPU v7x, 32 devices: a whole 2x2x4 slice. The times are simulated.
32 devices in a mesh: pw: 2 (over y), row: 4 (over z), col: 4 (over x, core).
Axes of the slice: x: 2, y: 2, z: 4, core: 2. Of those that a mesh axis runs over, the one named last changes fastest.
Arguments:
- pair_density: bfloat16 [2048, 2, 12288], P(('row', 'col'), None, 'pw'), may hold values from -0.25 to 0.25
- coulomb: float32 [12288], P('pw'), may hold values from 0.05 to 5
- valence_band: int32 [2048], P(('row', 'col')), may hold values from 0 to 511
- conduction_band: int32 [2048], P(('row', 'col')), may hold values from 0 to 31
- valence_energy: float32 [512], replicated, may hold values from -9 to -1
- conduction_energy: float32 [32], replicated, may hold values from 1 to 6
Outputs:
- hamiltonian: float32 [4, 4, 128, 2, 4, 4, 128], P('row', None, 'pw', None, None, 'col')
All inputs are finite; a program needn't handle non-finite values.
Results may differ from a plain program's by a relative error of at most 0.0003.
Values sent between devices are 32-bit elements; how exact they have to be, the bound alone decides.
A program may use at most 128 MiB of HBM per device.

v0:
```python
import jax
import jax.numpy as jnp
from jax import lax
from jax.sharding import PartitionSpec as P


def from_behind(block, axis, distance):
    devices = range(lax.axis_size(axis))
    route = [((i - distance) % len(devices), i) for i in devices]
    return lax.ppermute(block, axis, route)


def per_device(
    pair_density, coulomb, valence_band, conduction_band, valence_energy, conduction_energy
):
    tile_len = pair_density.shape[0]
    row_count = lax.axis_size("row")
    col_count = lax.axis_size("col")
    plane_count = lax.axis_size("pw")
    share_len = tile_len // plane_count
    row_here = lax.axis_index("row")
    col_here = lax.axis_index("col")
    plane_here = lax.axis_index("pw")

    def kept_block(block_ids):
        dist = jnp.remainder(block_ids - row_here, row_count)
        return (
            (dist == 0) | (2 * dist < row_count) | (2 * dist == row_count) & (row_here < block_ids)
        )

    scaled = jnp.sqrt(coulomb)[None, None, :] * pair_density.astype(jnp.float32)
    panel_rows = lax.all_gather(scaled, "col", axis=0, tiled=True)

    def columns(shard_rows):
        swapped = jnp.stack([shard_rows[:, 1, :], -shard_rows[:, 0, :]], axis=1)
        stacked = jnp.stack([shard_rows, swapped], axis=0)
        return lax.dot_general(
            panel_rows,
            stacked,
            (((1, 2), (2, 3)), ((), ())),
            precision=lax.Precision.HIGHEST,
            preferred_element_type=jnp.float32,
        )

    blocks = jnp.zeros((panel_rows.shape[0], 2, row_count, tile_len), jnp.float32)
    own_block = columns(scaled)
    blocks = lax.dynamic_update_slice_in_dim(blocks, own_block[:, :, None, :], row_here, 2)
    for dist in range(1, row_count // 2 + 1):
        ahead = from_behind(scaled, "row", -dist)
        target = jnp.remainder(row_here + dist, row_count)
        tile_block = columns(ahead)
        tile_block = jnp.where(kept_block(target), tile_block, 0.0)
        blocks = lax.dynamic_update_slice_in_dim(blocks, tile_block[:, :, None, :], target, 2)
    partial_value = blocks.reshape(col_count, tile_len, 2, row_count, tile_len)
    totals = lax.psum(partial_value, "pw")
    reduced = 2.0 * lax.dynamic_slice_in_dim(totals, plane_here * share_len, share_len, 1)
    outgoing = 2.0 * lax.dynamic_slice_in_dim(totals, plane_here * share_len, share_len, 4)
    outgoing = jnp.transpose(outgoing, (3, 0, 2, 1, 4)).reshape(
        row_count * col_count, 2, tile_len, share_len
    )
    incoming = lax.all_to_all(outgoing, ("row", "col"), split_axis=0, concat_axis=0, tiled=True)
    incoming = incoming.reshape(row_count, col_count, 2, tile_len, share_len)
    conjugate = jnp.array([1.0, -1.0], jnp.float32)
    mirrored = jnp.transpose(incoming, (1, 4, 2, 0, 3)) * conjugate[None, None, :, None, None]
    lower_tiles = jnp.logical_not(kept_block(jnp.arange(row_count, dtype=jnp.int32)))[
        None, None, None, :, None
    ]
    reduced = jnp.where(lower_tiles, mirrored, reduced)
    own_valence = lax.dynamic_slice_in_dim(valence_band, plane_here * share_len, share_len, 0)
    own_conduction = lax.dynamic_slice_in_dim(conduction_band, plane_here * share_len, share_len, 0)
    valence_ids = jnp.arange(valence_energy.shape[0], dtype=jnp.int32)
    conduction_ids = jnp.arange(conduction_energy.shape[0], dtype=jnp.int32)
    upper_level = jnp.sum(
        jnp.where(
            own_conduction[:, None] == conduction_ids[None, :], conduction_energy[None, :], 0.0
        ),
        axis=1,
    )
    lower_level = jnp.sum(
        jnp.where(own_valence[:, None] == valence_ids[None, :], valence_energy[None, :], 0.0),
        axis=1,
    )
    gap = upper_level - lower_level
    col_match = (jnp.arange(col_count, dtype=jnp.int32) == col_here)[:, None, None, None]
    row_match = (jnp.arange(row_count, dtype=jnp.int32) == row_here)[None, None, :, None]
    inner_match = (
        jnp.arange(tile_len, dtype=jnp.int32)[None, None, None, :]
        == plane_here * share_len + jnp.arange(share_len, dtype=jnp.int32)[None, :, None, None]
    )
    on_diagonal = col_match & row_match & inner_match
    addition = jnp.where(on_diagonal, gap[None, :, None, None], 0.0)
    result = reduced.at[:, :, 0].add(addition)
    return result.reshape(1, col_count, share_len, 2, row_count, 1, tile_len)


def solution(mesh):
    placed = (
        P(("row", "col"), None, "pw"),
        P("pw"),
        P(("row", "col")),
        P(("row", "col")),
        P(),
        P(),
    )
    return jax.shard_map(
        per_device,
        mesh=mesh,
        in_specs=placed,
        out_specs=P("row", None, "pw", None, None, "col", None),
        check_vma=False,
    )
```

profile of v0, /device:TPU:11, one launch (start us, length us, event | category | flops | bytes accessed | tf_op | source)
XLA Modules:
  0.0 611.5 jit_solution(16478427529188934011)
XLA Ops:
  6.5 0.0 all-gather.2.cloned.1.call-start
  6.5 0.7 sqrt.3
  7.3 8.2 %fusion.65 = (f32[1,128,2,6144]{3,1,2,0:T(8,128)}, f32[128,2,6144]{2,0,1:T(8,128)}) fusion(bf16[128,2,6144]{2,1,0:T(2,128)(2,1)} %param.9, f32[6144]{0:T(1024)S(1)} %sqrt.3), kind=kLoop, calls=%fused_computation.35 | loop fusion | flops 3145728 | bytes 15753216 | tf_op jit(solution)/shard_map/stack | solution.py:36
  15.5 0.0 all-gather.2.cloned.1.call-update
  15.5 0.0 all-reduce.2.cloned.1.call-start
  15.6 0.2 collective-permute-start
  15.8 2.3 collective-permute-start.1
  18.1 3.3 fusion.74
  21.4 3.7 maximum_bitcast_fusion
  25.1 127.3 %collective-permute-done = f32[128,2,6144]{2,0,1:T(8,128)} collective-permute-done((f32[128,2,6144]{2,0,1:T(8,128)}, f32[128,2,6144]{2,0,1:T(8,128)}, u32[]{:S(2)}, u32[]{:S(2)}) %collective-permute-start) | collective-permute-done | bytes 6291488 | tf_op jit(solution)/shard_map/ppermute | solution.py:10
  152.3 3.3 fusion.73
  155.6 3.0 maximum_bitcast_fusion.1
  158.6 263.9 %collective-permute-done.1 = f32[128,2,6144]{2,0,1:T(8,128)} collective-permute-done((f32[128,2,6144]{2,0,1:T(8,128)}, f32[128,2,6144]{2,0,1:T(8,128)}, u32[]{:S(2)}, u32[]{:S(2)}) %collective-permute-start.1) | collective-permute-done | bytes 6291488 | tf_op jit(solution)/shard_map/ppermute | solution.py:10
  422.5 3.3 fusion.72
  425.8 3.1 maximum_bitcast_fusion.2
  428.9 0.0 all-gather.2.cloned.1.call-done
  428.9 0.0 slice-start
  428.9 0.1 broadcast_in_dim.76
  429.0 0.0 slice-start.1
  429.0 0.0 slice-start.2
  429.1 0.0 slice-start.3
  429.1 0.0 slice-start.4
  429.1 0.0 slice-start.5
  429.1 24.3 %fusion.20 = f32[512,2,4,128]{3,0,2,1:T(8,128)S(1)} fusion(f32[512,2,4,128]{3,0,2,1:T(8,128)S(1)} %broadcast_in_dim.76, s32[]{:T(128)S(6)} %select_n.80, f32[1,128,2,6144]{3,1,2,0:T(8,128)} %maximum_bitcast_fusion, f32[1,128,2,6144]{3,1,2,0:T(8,128)} %get-tuple-element.23, f32[512,2,6144]{2,0,1:T(8,128)} %all-gather.2.cloned.1.call-done), kind=kOutput, calls=%fused_computation.24 | convolution fusion | flops 19330498560 | bytes 38273028 | tf_op jit(solution)/shard_map/dot_general | solution.py:37
  453.4 0.0 slice-done
  453.4 0.0 slice-done.1
  453.4 0.0 slice-done.2
  453.4 0.0 slice-done.3
  453.4 0.0 slice-done.4
  453.4 0.0 slice-done.5
  453.5 22.7 %fusion.60 = f32[512,2,4,128]{3,0,2,1:T(8,128)S(1)} fusion(f32[512,2,4,128]{3,0,2,1:T(8,128)S(1)} %fusion.20, s32[]{:T(128)S(6)} %select_n.85, f32[1,128,2,6144]{3,1,2,0:T(8,128)} %maximum_bitcast_fusion.1, f32[1,128,2,6144]{3,1,2,0:T(8,128)} %bitcast.7, f32[512,2,6144]{2,0,1:T(8,128)S(1)} %bitcast.90, pred[]{:T(512)S(6)} %or.29), kind=kOutput, calls=%fused_computation.32 | convolution fusion | flops 19330629632 | bytes 38273028 | tf_op jit(solution)/shard_map/dot_general | solution.py:37
  476.2 22.7 %fusion.45 = f32[512,2,4,128]{3,0,2,1:T(8,128)S(1)} fusion(f32[512,2,4,128]{3,0,2,1:T(8,128)S(1)} %fusion.60, s32[]{:T(128)S(6)} %select_n.90, f32[1,128,2,6144]{3,1,2,0:T(8,128)} %maximum_bitcast_fusion.2, f32[1,128,2,6144]{3,1,2,0:T(8,128)} %bitcast.13, f32[512,2,6144]{2,0,1:T(8,128)S(1)} %bitcast.90, pred[]{:T(512)S(6)} %or.31), kind=kOutput, calls=%fused_computation.29 | convolution fusion | flops 19330629632 | bytes 38273028 | tf_op jit(solution)/shard_map/dot_general | solution.py:37
  498.9 0.0 copy-start
  498.9 0.0 copy-start.3
  498.9 0.0 copy-start.4
  498.9 0.0 copy-start.5
  498.9 0.0 copy-start.1
  498.9 0.0 copy-start.2
  499.0 1.2 copy-done
  500.2 0.0 all-reduce.2.cloned.1.call-update
  500.2 65.6 %all-reduce.2.cloned.1.call-done = f32[4,128,2,4,128]{4,1,0,3,2:T(8,128)} async-done(((f32[4,128,2,4,128]{4,1,0,3,2:T(8,128)}), f32[4,128,2,4,128]{4,1,0,3,2:T(8,128)}) %all-reduce.2.cloned.1.call-update) | async-done | bytes 2097168 | tf_op jit(solution)/shard_map/psum | solution.py:55
  565.8 2.2 multiply_bitcast_fusion
  568.0 1.6 copy.29
  569.6 6.4 %all-to-all-start = ((f32[16,2,128,64]{2,3,1,0:T(8,128)}), f32[16,2,128,64]{2,3,1,0:T(8,128)S(1)}, u32[]{:S(2)}, u32[]{:S(2)}) async-start(f32[16,2,128,64]{2,3,1,0:T(8,128)} %bitcast.21), calls=%async_computation | async-start | bytes 2097152 | tf_op jit(solution)/shard_map/all_to_all | solution.py:61
  576.0 0.0 copy-done.3
  576.0 0.1 dynamic_slice.15
  576.0 0.0 copy-done.4
  576.0 0.1 dynamic_slice.14
  576.1 0.0 copy-done.5
  576.1 0.1 select_reduce_fusion.1
  576.2 0.0 copy-done.1
  576.2 0.2 select_reduce_fusion
  576.5 0.1 broadcast_and_fusion
  576.5 0.1 iota_compare_fusion.1
  576.6 24.2 %all-to-all-done = f32[16,2,128,64]{2,3,1,0:T(8,128)S(1)} async-done(((f32[16,2,128,64]{2,3,1,0:T(8,128)}), f32[16,2,128,64]{2,3,1,0:T(8,128)S(1)}, u32[]{:S(2)}, u32[]{:S(2)}) %all-to-all-start) | async-done | bytes 1048608 | tf_op jit(solution)/shard_map/all_to_all | solution.py:61
  600.8 0.0 copy-done.2
  600.8 1.5 bitcast_select_fusion
  602.3 0.1 copy.46
  602.4 0.2 fusion.67
  602.6 2.0 copy.32
  (5 shorter events, 0.0 us)
Async XLA Ops:
  6.5 422.4 %all-gather.2.cloned.1.call-start = ((), (), s32[]{:S(2)}) async-start(), calls=%async_computation.1 | async-start | bytes 31457280 | tf_op jit(solution)/shard_map/all_gather | solution.py:32
  15.5 550.3 %all-reduce.2.cloned.1.call-start = ((), (), s32[]{:S(2)}) async-start(), calls=%async_computation.2 | async-start | bytes 4194304 | tf_op jit(solution)/shard_map/psum | solution.py:55
  15.6 136.7 %collective-permute-start = (f32[128,2,6144]{2,0,1:T(8,128)}, f32[128,2,6144]{2,0,1:T(8,128)}, u32[]{:S(2)}, u32[]{:S(2)}) collective-permute-start(f32[128,2,6144]{2,0,1:T(8,128)} %get-tuple-element.24), channel_id=1, source_target_pairs={{4,0},{8,4},{12,8},{0,12},{5,1},{9,5},{13,9},{1,13},{6,2},{10,6},{... | collective-permute-start | bytes 18874376 | tf_op jit(solution)/shard_map/ppermute | solution.py:10
  15.8 406.7 %collective-permute-start.1 = (f32[128,2,6144]{2,0,1:T(8,128)}, f32[128,2,6144]{2,0,1:T(8,128)}, u32[]{:S(2)}, u32[]{:S(2)}) collective-permute-start(f32[128,2,6144]{2,0,1:T(8,128)} %get-tuple-element.24), channel_id=1, source_target_pairs={{8,0},{12,4},{0,8},{4,12},{9,1},{13,5},{1,9},{5,13},{10,2},{14,6},... | collective-permute-start | bytes 18874376 | tf_op jit(solution)/shard_map/ppermute | solution.py:10
  428.9 24.5 %slice-start = ((s8[25165824]{0:T(1024)(128)(4,1)}), s8[4194304]{0:T(1024)(128)(4,1)S(1)}, s32[]{:S(2)}) async-start(s8[25165824]{0:T(1024)(128)(4,1)} %bitcast.89), calls=%async_computation.3 | async-start | bytes 8388608
  429.0 24.4 %slice-start.1 = ((s8[25165824]{0:T(1024)(128)(4,1)}), s8[4194304]{0:T(1024)(128)(4,1)S(1)}, s32[]{:S(2)}) async-start(s8[25165824]{0:T(1024)(128)(4,1)} %bitcast.89), calls=%async_computation.4 | async-start | bytes 8388608
  429.0 24.4 %slice-start.2 = ((s8[25165824]{0:T(1024)(128)(4,1)}), s8[4194304]{0:T(1024)(128)(4,1)S(1)}, s32[]{:S(2)}) async-start(s8[25165824]{0:T(1024)(128)(4,1)} %bitcast.89), calls=%async_computation.5 | async-start | bytes 8388608
  429.1 24.4 %slice-start.3 = ((s8[25165824]{0:T(1024)(128)(4,1)}), s8[4194304]{0:T(1024)(128)(4,1)S(1)}, s32[]{:S(2)}) async-start(s8[25165824]{0:T(1024)(128)(4,1)} %bitcast.89), calls=%async_computation.6 | async-start | bytes 8388608
  429.1 24.4 %slice-start.4 = ((s8[25165824]{0:T(1024)(128)(4,1)}), s8[4194304]{0:T(1024)(128)(4,1)S(1)}, s32[]{:S(2)}) async-start(s8[25165824]{0:T(1024)(128)(4,1)} %bitcast.89), calls=%async_computation.7 | async-start | bytes 8388608
  429.1 24.4 %slice-start.5 = ((s8[25165824]{0:T(1024)(128)(4,1)}), s8[4194304]{0:T(1024)(128)(4,1)S(1)}, s32[]{:S(2)}) async-start(s8[25165824]{0:T(1024)(128)(4,1)} %bitcast.89), calls=%async_computation.8 | async-start | bytes 8388608
  498.9 1.3 copy-start
  498.9 77.1 %copy-start.3 = (s32[128]{0:T(128)S(1)}, s32[128]{0:T(128)}, u32[]{:S(2)}) copy-start(s32[128]{0:T(128)} %param.11) | copy-start | bytes 1540
  498.9 77.1 %copy-start.4 = (s32[128]{0:T(128)S(1)}, s32[128]{0:T(128)}, u32[]{:S(2)}) copy-start(s32[128]{0:T(128)} %param.12) | copy-start | bytes 1540
  498.9 77.2 %copy-start.5 = (f32[32]{0:T(128)S(1)}, f32[32]{0:T(128)}, u32[]{:S(2)}) copy-start(f32[32]{0:T(128)} %param.14) | copy-start | bytes 388
  498.9 77.3 %copy-start.1 = (f32[512]{0:T(512)S(1)}, f32[512]{0:T(512)}, u32[]{:S(2)}) copy-start(f32[512]{0:T(512)} %param.13) | copy-start | bytes 6148
  498.9 101.9 %copy-start.2 = (f32[2]{0:T(128)S(1)}, f32[2]{0:T(128)}, u32[]{:S(2)}) copy-start(f32[2]{0:T(128)} %constant.93.clone) | copy-start | bytes 28
  569.6 31.2 %all-to-all-start = ((f32[16,2,128,64]{2,3,1,0:T(8,128)}), f32[16,2,128,64]{2,3,1,0:T(8,128)S(1)}, u32[]{:S(2)}, u32[]{:S(2)}) async-start(f32[16,2,128,64]{2,3,1,0:T(8,128)} %bitcast.21), calls=%async_computation | async-start | bytes 2097152 | tf_op jit(solution)/shard_map/all_to_all | solution.py:61
Sparse Core Ops, SparseCore 0:
  15.6 154.4 all-gather.1
  500.3 65.4 all-reduce.1
where the time goes:
time: 612 us; the launch traced here: 611 us
  waiting for transfers between devices  481 us (79%)
  matrix products  69.7 us (11%)
  other arithmetic  32.2 us (5%)
  between operations  13.7 us (2%)
  starting transfers between devices  8.95 us (1%)
    ppermute x2, waiting for transfers between devices, from_behind(): return lax.ppermute(block, axis, route)  391 us
    dot_general x3, matrix products, columns(): lax.dot_general(panel_rows, stacked, (((1, 2), (2, 3)), ((), ())), precis...  69.7 us
    psum x1, waiting for transfers between devices, per_device(): totals = lax.psum(partial_value, 'pw')  65.6 us
    all_to_all x1, waiting for transfers between devices, per_device(): lax.all_to_all(outgoing, ('row', 'col'), split_axis=0, concat_axis=0, til...  24.2 us
    another operation x4, other arithmetic, columns(): stacked = jnp.stack([shard_rows, swapped], axis=0)  17.9 us
  transfers between devices with their start and end apart: 5, of which 4 were waited for; matrix products, arithmetic and copies ran while one was open for 3% of the time, Pallas kernels for 0%

commit v1 on v0

v1 whole, which is shorter than its diff:
```python
import functools
import jax
import jax.numpy as jnp
from jax import lax
from jax.experimental import pallas as pl
from jax.experimental.pallas import tpu as pltpu
from jax.sharding import PartitionSpec as P

MESH = pl.DeviceIdType.MESH


def piece_width(depth):
    for width in (768, 512, 256):
        if depth % (2 * width) == 0:
            return width
    return 128


def kernel(
    rows, pieces, x_ref, c_ref, o_ref, panel, same, other, acc,
    p_recv, same_recv, other_recv, own_send, in_send, out_send,
):
    half = pieces // 2
    mid = rows // 2
    ahead = min(2, half)
    z = lax.axis_index("row")
    b = lax.axis_index("col")
    core = b + 1 - 2 * (b % 2)
    beside = (b + 2) % 4
    opposite = 3 - b
    side = z // mid
    m = z + side * (rows - 1 - 2 * z)
    step_in = 1 - 2 * side
    z_in = z + step_in
    z_out = z - step_in
    innermost = m == mid - 1
    cross_count = half * mid
    outer_count = 2 * half * m
    inner_sends = jnp.where(innermost, half * (m + 1), 2 * half * (m + 1))

    barrier = pltpu.get_barrier_semaphore()
    pl.semaphore_signal(barrier, inc=1, device_id={"col": core}, device_id_type=MESH)
    pl.semaphore_signal(barrier, inc=1, device_id={"col": beside}, device_id_type=MESH)
    pl.semaphore_signal(barrier, inc=1, device_id={"row": z_in}, device_id_type=MESH)

    @pl.when(m > 0)
    def _():
        pl.semaphore_signal(barrier, inc=1, device_id={"row": z_out}, device_id_type=MESH)
        pl.semaphore_wait(barrier, 4)

    @pl.when(m == 0)
    def _():
        pl.semaphore_wait(barrier, 3)

    def copy(src, dst, send, recv, where):
        return pltpu.make_async_remote_copy(
            src_ref=src, dst_ref=dst, send_sem=send, recv_sem=recv,
            device_id=where, device_id_type=MESH,
        )

    def arrived(slot, recv):
        copy(slot, slot, own_send.at[0, 0], recv, {"col": core}).wait_recv()

    def order(i):
        return (i + half) % pieces

    def send_own(i):
        q = order(i)
        copy(x_ref.at[q], panel.at[0, q], own_send.at[0, q], p_recv.at[0, q], {"col": core}).start()
        copy(x_ref.at[q], panel.at[1, q], own_send.at[1, q], p_recv.at[1, q], {"col": beside}).start()

    def send_inward(s):
        crossing = s < half * (m + 1)
        rest = jnp.where(crossing, s, s - half * (m + 1))
        back = rest // half
        chunk = m - back
        q = rest % half + jnp.where(crossing, 0, half)
        where = {"row": z_in}

        @pl.when(innermost & (back == 0))
        def _():
            copy(x_ref.at[q], other.at[chunk, q], in_send.at[s], other_recv.at[chunk, q], where).start()

        @pl.when(innermost & (back > 0))
        def _():
            copy(same.at[chunk, q], other.at[chunk, q], in_send.at[s], other_recv.at[chunk, q], where).start()

        @pl.when(jnp.logical_not(innermost) & (back == 0))
        def _():
            copy(x_ref.at[q], same.at[chunk, q], in_send.at[s], same_recv.at[chunk, q], where).start()

        if mid > 2:
            @pl.when(jnp.logical_not(innermost) & (back > 0))
            def _():
                copy(same.at[chunk, q], same.at[chunk, q], in_send.at[s], same_recv.at[chunk, q], where).start()

    def outer_arrival(u):
        crossing = u < half * m
        rest = jnp.where(crossing, u, u - half * m)
        return m - 1 - rest // half, rest % half + jnp.where(crossing, 0, half)

    def multiply(chunk, q, target):
        weighted = chunk[...] * c_ref[q]
        high = weighted.astype(jnp.bfloat16)
        low = (weighted - high.astype(jnp.float32)).astype(jnp.bfloat16)
        blocks = (x_ref.at[q], panel.at[0, q], panel.at[1, q], panel.at[2, q])
        dims = (((1,), (1,)), ((), ()))
        for block, a in zip(blocks, (b, core, beside, opposite)):
            left = block[...].astype(jnp.bfloat16)
            acc[target, a] += lax.dot_general(
                left, high, dims, preferred_element_type=jnp.float32
            ) + lax.dot_general(left, low, dims, preferred_element_type=jnp.float32)

    for i in range(ahead):
        send_own(i)
        send_inward(i)

    def clear(i, carry):
        acc[i // 4, i % 4] = jnp.zeros(acc.shape[2:], jnp.float32)
        return carry

    lax.fori_loop(0, rows * 4, clear, 0)
    lag = mid - 1 - m

    def step(t, carry):
        v = t - lag
        inner_here = (v >= 0) & (v < cross_count)
        v = jnp.clip(v, 0, cross_count - 1)
        inner_chunk, inner_q = mid - 1 - v // half, v % half

        @pl.when(t < outer_count)
        def _():
            chunk, q = outer_arrival(t)
            arrived(same.at[chunk, q], same_recv.at[chunk, q])

        @pl.when(t + ahead < inner_sends)
        def _():
            send_inward(t + ahead)

        @pl.when(t + ahead < pieces)
        def _():
            send_own(t + ahead)

        @pl.when(inner_here)
        def _():
            arrived(other.at[inner_chunk, inner_q], other_recv.at[inner_chunk, inner_q])

        @pl.when(inner_here & (m > 0))
        def _():
            copy(
                other.at[inner_chunk, inner_q], other.at[inner_chunk, inner_q],
                out_send.at[v], other_recv.at[inner_chunk, inner_q], {"row": z_out},
            ).start()

        @pl.when(t < pieces)
        def _():
            q = order(t)
            arrived(panel.at[1, q], p_recv.at[1, q])
            copy(
                panel.at[1, q], panel.at[2, q], own_send.at[2, q], p_recv.at[2, q], {"col": core}
            ).start()
            arrived(panel.at[0, q], p_recv.at[0, q])

        @pl.when((t >= 1) & (t <= pieces))
        def _():
            q = order(t - 1)
            arrived(panel.at[2, q], p_recv.at[2, q])
            multiply(x_ref.at[q], q, z)

        @pl.when((t >= half + 1) & (t - half - 1 < half * m))
        def _():
            chunk, q = outer_arrival(t - half - 1)
            multiply(same.at[chunk, q], q, chunk + side * (rows - 1 - 2 * chunk))

        @pl.when((t >= half * m) & (t < outer_count))
        def _():
            chunk, q = outer_arrival(t)
            multiply(same.at[chunk, q], q, chunk + side * (rows - 1 - 2 * chunk))

        w = t - 1 - lag

        @pl.when((w >= 0) & (w < cross_count))
        def _():
            chunk, q = mid - 1 - w // half, w % half
            multiply(other.at[chunk, q], q + half, chunk + (1 - side) * (rows - 1 - 2 * chunk))

        return carry

    steps = max(pieces + 1, cross_count + mid, 2 * half * (mid - 1))
    lax.fori_loop(0, steps, step, 0)

    def finish(i, carry):
        s, a = i // 4, i % 4
        n = acc.shape[2] // 2
        o_ref[s, a, 0] = 2.0 * (acc[s, a, :n, :n] + acc[s, a, n:, n:])
        o_ref[s, a, 1] = 2.0 * (acc[s, a, :n, n:] - acc[s, a, n:, :n])
        return carry

    lax.fori_loop(0, rows * 4, finish, 0)

    def left(send):
        copy(x_ref.at[0], panel.at[0, 0], send, p_recv.at[0, 0], {"col": core}).wait_send()

    def drain_own(i, carry):
        left(own_send.at[0, i])
        left(own_send.at[1, i])
        left(own_send.at[2, i])
        return carry

    lax.fori_loop(0, pieces, drain_own, 0)

    def drain_in(i, carry):
        @pl.when(i < inner_sends)
        def _():
            left(in_send.at[i])

        return carry

    lax.fori_loop(0, 2 * cross_count, drain_in, 0)

    @pl.when(m > 0)
    def _():
        def drain_out(i, carry):
            left(out_send.at[i])
            return carry

        lax.fori_loop(0, cross_count, drain_out, 0)


def partial_tiles(x, c, row_count):
    pieces, height, width = x.shape
    half, mid = pieces // 2, row_count // 2
    return pl.pallas_call(
        functools.partial(kernel, row_count, pieces),
        out_shape=jax.ShapeDtypeStruct((row_count, 4, 2, height // 2, height // 2), jnp.float32),
        in_specs=[pl.BlockSpec(memory_space=pltpu.VMEM)] * 2,
        out_specs=pl.BlockSpec(memory_space=pltpu.VMEM),
        scratch_shapes=[
            pltpu.VMEM((3, pieces, height, width), jnp.float32),
            pltpu.VMEM((max(mid - 1, 1), pieces, height, width), jnp.float32),
            pltpu.VMEM((mid, half, height, width), jnp.float32),
            pltpu.VMEM((row_count, 4, height, height), jnp.float32),
            pltpu.SemaphoreType.DMA((3, pieces)),
            pltpu.SemaphoreType.DMA((max(mid - 1, 1), pieces)),
            pltpu.SemaphoreType.DMA((mid, half)),
            pltpu.SemaphoreType.DMA((3, pieces)),
            pltpu.SemaphoreType.DMA((2 * half * mid,)),
            pltpu.SemaphoreType.DMA((half * mid,)),
        ],
        compiler_params=pltpu.CompilerParams(
            collective_id=0, has_side_effects=True, vmem_limit_bytes=56 * 2**20
        ),
    )(x, c)


def per_device(
    pair_density, coulomb, valence_band, conduction_band, valence_energy, conduction_energy
):
    tile_len, _, depth = pair_density.shape
    row_count = lax.axis_size("row")
    col_count = lax.axis_size("col")
    plane_count = lax.axis_size("pw")
    share_len = tile_len // plane_count
    row_here = lax.axis_index("row")
    col_here = lax.axis_index("col")
    plane_here = lax.axis_index("pw")
    assert col_count == 4 and row_count % 2 == 0

    width = piece_width(depth)
    pieces = depth // width
    far_side = row_here >= row_count // 2

    def from_side(array):
        return jnp.where(far_side, jnp.roll(array, pieces // 2, axis=0), array)

    x = jnp.transpose(pair_density.reshape(tile_len, 2, pieces, width), (2, 1, 0, 3))
    x = from_side(x.reshape(pieces, 2 * tile_len, width)).astype(jnp.float32)
    c = from_side(coulomb.reshape(pieces, 1, width))
    blocks = partial_tiles(x, c, row_count)

    def shares(plane):
        rows = lax.dynamic_slice_in_dim(blocks, plane * share_len, share_len, 3)
        cols = lax.dynamic_slice_in_dim(blocks, plane * share_len, share_len, 4)
        rows = jnp.transpose(rows, (1, 3, 2, 0, 4))
        cols = jnp.transpose(cols, (0, 1, 2, 4, 3))
        return rows, cols

    direct, outgoing = shares(plane_here)
    for distance in range(1, plane_count):
        route = [(i, (i + distance) % plane_count) for i in range(plane_count)]
        rows, cols = shares(jnp.remainder(plane_here + distance, plane_count))
        outgoing = outgoing + lax.ppermute(cols, "pw", route)
        direct = direct + lax.ppermute(rows, "pw", route)
    outgoing = outgoing.reshape(row_count * col_count, 2, share_len, tile_len)
    incoming = lax.all_to_all(outgoing, ("row", "col"), split_axis=0, concat_axis=0, tiled=True)
    incoming = incoming.reshape(row_count, col_count, 2, share_len, tile_len)
    conjugate = jnp.array([1.0, -1.0], jnp.float32)
    mirrored = jnp.transpose(incoming, (1, 3, 2, 0, 4)) * conjugate[None, None, :, None, None]
    elsewhere = (jnp.arange(row_count, dtype=jnp.int32) != row_here)[None, None, None, :, None]
    reduced = direct + jnp.where(elsewhere, mirrored, 0.0)
    own_valence = lax.dynamic_slice_in_dim(valence_band, plane_here * share_len, share_len, 0)
    own_conduction = lax.dynamic_slice_in_dim(conduction_band, plane_here * share_len, share_len, 0)
    valence_ids = jnp.arange(valence_energy.shape[0], dtype=jnp.int32)
    conduction_ids = jnp.arange(conduction_energy.shape[0], dtype=jnp.int32)
    upper_level = jnp.sum(
        jnp.where(
            own_conduction[:, None] == conduction_ids[None, :], conduction_energy[None, :], 0.0
        ),
        axis=1,
    )
    lower_level = jnp.sum(
        jnp.where(own_valence[:, None] == valence_ids[None, :], valence_energy[None, :], 0.0),
        axis=1,
    )
    gap = upper_level - lower_level
    col_match = (jnp.arange(col_count, dtype=jnp.int32) == col_here)[:, None, None, None, None]
    row_match = (jnp.arange(row_count, dtype=jnp.int32) == row_here)[None, None, None, :, None]
    real_match = (jnp.arange(2, dtype=jnp.int32) == 0)[None, None, :, None, None]
    inner_match = (
        jnp.arange(tile_len, dtype=jnp.int32)[None, None, None, None, :]
        == plane_here * share_len
        + jnp.arange(share_len, dtype=jnp.int32)[None, :, None, None, None]
    )
    on_diagonal = col_match & row_match & real_match & inner_match
    result = reduced + jnp.where(on_diagonal, gap[None, :, None, None, None], 0.0)
    return result.reshape(1, col_count, share_len, 2, row_count, 1, tile_len)


def solution(mesh):
    placed = (
        P(("row", "col"), None, "pw"),
        P("pw"),
        P(("row", "col")),
        P(("row", "col")),
        P(),
        P(),
    )
    return jax.shard_map(
        per_device,
        mesh=mesh,
        in_specs=placed,
        out_specs=P("row", None, "pw", None, None, "col", None),
        check_vma=False,
    )
```

time: 612 us -> 258 us (0.42)
  waiting for transfers between devices: 481 us -> 44.1 us
  Pallas kernels: 0 us -> 158 us
  matrix products: 69.7 us -> 0 us
  other arithmetic: 32.2 us -> 11.4 us
  local copies, waits for them, and re-layouts: 6.01 us -> 25.2 us
  between operations: 13.7 us -> 0.12 us
  starting transfers between devices: 8.95 us -> 17 us
    ppermute x2, waiting for transfers between devices: 391 us -> 44.1 us  [the longest x1 22.7 us: per_device(): direct = direct + lax.ppermute(rows, 'pw', route)]
    pallas_call x0 -> x1, Pallas kernels: none -> 158 us  [partial_tiles(): pl.pallas_call(functools.partial(kernel, row_count, pieces), out_shape=ja...]
    dot_general x3 -> x0, matrix products: 69.7 us -> none  [columns(): lax.dot_general(panel_rows, stacked, (((1, 2), (2, 3)), ((), ())), precis...]
    psum x1 -> x0, waiting for transfers between devices: 65.6 us -> none  [per_device(): totals = lax.psum(partial_value, 'pw')]
    all_to_all x1, waiting for transfers between devices: 24.2 us -> 0.01 us  [per_device(): lax.all_to_all(outgoing, ('row', 'col'), split_axis=0, concat_axis=0, til...]
    another operation x4 -> x0, other arithmetic: 17.9 us -> none  [columns(): stacked = jnp.stack([shard_rows, swapped], axis=0)]
    reshape x0 -> x4, local copies, waits for them, and re-layouts: none -> 16.1 us  [the longest x2 10.9 us: per_device(): pair_density.reshape(tile_len, 2, pieces, width)]
    slice x3 -> x0, other arithmetic: 9.9 us -> none  [columns(): swapped = jnp.stack([shard_rows[:, 1, :], -shard_rows[:, 0, :]], axis=1)]
  transfers between devices with their start and end apart: 5 -> 3, of which waited for: 4 -> 2; matrix products, arithmetic and copies ran while one was open for 3% -> 1% of each run, Pallas kernels for 0% -> 0%
where the time goes in v1:
time: 258 us; the launch traced here: 256 us
  Pallas kernels  158 us (61%)
  waiting for transfers between devices  44.1 us (17%)
  local copies, waits for them, and re-layouts  25.2 us (10%)
  starting transfers between devices  17 us (7%)
  other arithmetic  11.4 us (4%)
    pallas_call x1, Pallas kernels, partial_tiles(): pl.pallas_call(functools.partial(kernel, row_count, pieces), out_shape=ja...  158 us
    ppermute x1, waiting for transfers between devices, per_device(): direct = direct + lax.ppermute(rows, 'pw', route)  22.7 us
    ppermute x1, waiting for transfers between devices, per_device(): outgoing = outgoing + lax.ppermute(cols, 'pw', route)  21.3 us
    all_to_all x1, starting transfers between devices, per_device(): lax.all_to_all(outgoing, ('row', 'col'), split_axis=0, concat_axis=0, til...  14.4 us
    reshape x2, local copies, waits for them, and re-layouts, per_device(): pair_density.reshape(tile_len, 2, pieces, width)  10.9 us
  transfers between devices with their start and end apart: 3, of which 2 were waited for; matrix products, arithmetic and copies ran while one was open for 1% of the time, Pallas kernels for 0%

profile of v1, /device:TPU:11, one launch (start us, length us, event | category | flops | bytes accessed | tf_op | source)
XLA Modules:
  0.0 255.8 jit_solution(13698021739156931236)
XLA Ops:
  0.0 8.0 %reshape.175 = bf16[128,2,8,768]{3,2,1,0:T(8,128)(2,1)} reshape(bf16[128,2,6144]{2,1,0:T(2,128)(2,1)} %param.7) | data formatting | bytes 6291456 | tf_op jit(solution)/shard_map/reshape | solution.py:276
  8.0 2.9 %copy.23 = bf16[128,2,8,768]{3,0,1,2:T(8,128)(2,1)S(1)} copy(bf16[128,2,8,768]{3,2,1,0:T(8,128)(2,1)} %reshape.175) | data formatting | bytes 6291456 | tf_op jit(solution)/shard_map/reshape | solution.py:276
  10.9 0.0 copy-start.1
  10.9 1.9 fusion.4
  12.8 0.0 copy-done.1
  12.8 5.0 %fusion.x_ref = f32[8,256,768]{2,1,0:T(8,128)} fusion(bf16[4,256,768]{2,1,0:T(8,128)(2,1)} %bitcast.33, bf16[4,256,768]{2,1,0:T(8,128)(2,1)} %bitcast.32, bf16[128,2,8,768]{3,0,1,2:T(8,128)(2,1)S(1)} %copy.23, pred[]{:T(512)S(6)} %ge.3), kind=kLoop, calls=%fused_computation.1 | loop fusion | flops 4718592 | bytes 12582913 | tf_op jit(solution)/shard_map/convert_element_type | solution.py:277
  17.9 0.6 broadcast_select_fusion.c_ref
  18.5 158.0 %shard_map.73 = f32[4,4,2,128,128]{4,3,2,1,0:T(8,128)} custom-call(f32[8,256,768]{2,1,0:T(8,128)} %fusion.x_ref, f32[8,1,768]{2,1,0:T(1,128)} %broadcast_select_fusion.c_ref), custom_call_target="tpu_custom_call" | custom-call | tf_op jit(solution)/shard_map/pallas_call | solution.py:233
  176.5 2.2 dynamic-slice_bitcast_fusion
  178.7 0.6 copy.17
  179.3 0.0 copy-start
  179.3 1.3 collective-permute-start.1
  180.6 21.3 %collective-permute-done.1 = f32[4,4,2,64,128]{4,3,2,1,0:T(8,128)} collective-permute-done((f32[4,4,2,64,128]{4,3,2,1,0:T(8,128)S(1)}, f32[4,4,2,64,128]{4,3,2,1,0:T(8,128)}, u32[]{:S(2)}, u32[]{:S(2)}) %collective-permute-start.1) | collective-permute-done | bytes 1048608 | tf_op jit(solution)/shard_map/ppermute | solution.py:292
  202.0 3.2 %copy.18 = f32[4,4,2,64,128]{3,4,2,1,0:T(8,128)} copy(f32[4,4,2,64,128]{4,3,2,1,0:T(8,128)} %collective-permute-done.1) | data formatting | bytes 2097152 | tf_op jit(solution)/shard_map/ppermute | solution.py:292
  205.1 0.0 copy-done
  205.1 3.5 %bitcast_add_fusion = f32[4,4,2,64,128]{3,4,2,1,0:T(8,128)} fusion(f32[4,4,2,64,128]{3,4,2,1,0:T(8,128)} %copy.18, f32[4,4,2,128,128]{4,3,2,1,0:T(8,128)S(1)} %copy-done, s32[]{:T(128)S(6)} %select_n.56), kind=kLoop, calls=%fused_computation.2 | loop fusion | flops 262144 | bytes 3145732 | tf_op jit(solution)/shard_map/add | solution.py:292
  208.7 3.2 %copy.19 = f32[16,2,64,128]{3,2,1,0:T(8,128)} copy(f32[16,2,64,128]{2,3,1,0:T(8,128)} %bitcast.31) | data formatting | bytes 2097152 | tf_op jit(solution)/shard_map/reshape | solution.py:294
  211.8 0.0 copy-start.4
  211.8 0.0 copy-start.5
  211.8 0.0 copy-start.6
  211.8 0.0 copy-start.2
  211.9 0.0 copy-start.3
  211.9 14.4 %all-to-all-start = ((f32[16,2,64,128]{3,2,1,0:T(8,128)}), f32[16,2,64,128]{3,2,1,0:T(8,128)S(1)}, u32[]{:S(2)}, u32[]{:S(2)}) async-start(f32[16,2,64,128]{3,2,1,0:T(8,128)} %copy.19), calls=%async_computation | async-start | bytes 2097152 | tf_op jit(solution)/shard_map/all_to_all | solution.py:295
  226.3 1.0 dynamic-slice_bitcast_fusion.1
  227.3 1.2 collective-permute-start
  228.6 0.0 copy-done.4
  228.6 0.1 dynamic_slice.22
  228.6 0.0 copy-done.5
  228.6 0.1 dynamic_slice.23
  228.7 0.0 copy-done.6
  228.7 0.1 select_reduce_fusion.1
  228.8 0.0 copy-done.2
  228.8 0.2 select_reduce_fusion
  229.0 0.1 broadcast_and_fusion.1
  229.1 0.1 broadcast_and_fusion
  229.2 0.1 iota_compare_fusion.1
  229.3 22.7 %collective-permute-done = f32[4,64,2,4,128]{4,1,2,0,3:T(8,128)} collective-permute-done((f32[4,64,2,4,128]{4,1,2,0,3:T(8,128)}, f32[4,64,2,4,128]{4,1,2,0,3:T(8,128)}, u32[]{:S(2)}, u32[]{:S(2)}) %collective-permute-start) | collective-permute-done | bytes 1048608 | tf_op jit(solution)/shard_map/ppermute | solution.py:293
  252.0 0.0 all-to-all-done
  252.0 0.0 copy-done.3
  252.0 1.7 fusion.2
  253.7 2.0 copy.20
  (6 shorter events, 0.0 us)
Async XLA Ops:
  10.9 1.9 copy-start.1
  179.3 25.8 %copy-start = (f32[4,4,2,128,128]{4,3,2,1,0:T(8,128)S(1)}, f32[4,4,2,128,128]{4,3,2,1,0:T(8,128)}, u32[]{:S(2)}) copy-start(f32[4,4,2,128,128]{4,3,2,1,0:T(8,128)} %shard_map.73) | copy-start | bytes 6291460
  179.3 22.6 %collective-permute-start.1 = (f32[4,4,2,64,128]{4,3,2,1,0:T(8,128)S(1)}, f32[4,4,2,64,128]{4,3,2,1,0:T(8,128)}, u32[]{:S(2)}, u32[]{:S(2)}) collective-permute-start(f32[4,4,2,64,128]{4,3,2,1,0:T(8,128)S(1)} %copy.17), channel_id=1, source_target_pairs={{0,16},{16,0},{1,17},{17,1},{2,18},{18,2},{3,19},{19,3},{4,20},{20... | collective-permute-start | bytes 3145736 | tf_op jit(solution)/shard_map/ppermute | solution.py:292
  211.8 16.7 %copy-start.4 = (s32[128]{0:T(128)S(1)}, s32[128]{0:T(128)}, u32[]{:S(2)}) copy-start(s32[128]{0:T(128)} %param.10) | copy-start | bytes 1540
  211.8 16.8 %copy-start.5 = (s32[128]{0:T(128)S(1)}, s32[128]{0:T(128)}, u32[]{:S(2)}) copy-start(s32[128]{0:T(128)} %param.9) | copy-start | bytes 1540
  211.8 16.9 %copy-start.6 = (f32[32]{0:T(128)S(1)}, f32[32]{0:T(128)}, u32[]{:S(2)}) copy-start(f32[32]{0:T(128)} %param.12) | copy-start | bytes 388
  211.8 17.0 %copy-start.2 = (f32[512]{0:T(512)S(1)}, f32[512]{0:T(512)}, u32[]{:S(2)}) copy-start(f32[512]{0:T(512)} %param.11) | copy-start | bytes 6148
  211.9 40.2 %copy-start.3 = (f32[2]{0:T(128)S(1)}, f32[2]{0:T(128)}, u32[]{:S(2)}) copy-start(f32[2]{0:T(128)} %constant.37.clone) | copy-start | bytes 28
  211.9 40.1 %all-to-all-start = ((f32[16,2,64,128]{3,2,1,0:T(8,128)}), f32[16,2,64,128]{3,2,1,0:T(8,128)S(1)}, u32[]{:S(2)}, u32[]{:S(2)}) async-start(f32[16,2,64,128]{3,2,1,0:T(8,128)} %copy.19), calls=%async_computation | async-start | bytes 2097152 | tf_op jit(solution)/shard_map/all_to_all | solution.py:295
  227.3 24.7 %collective-permute-start = (f32[4,64,2,4,128]{4,1,2,0,3:T(8,128)}, f32[4,64,2,4,128]{4,1,2,0,3:T(8,128)}, u32[]{:S(2)}, u32[]{:S(2)}) collective-permute-start(f32[4,64,2,4,128]{4,1,2,0,3:T(8,128)} %dynamic-slice_bitcast_fusion.1), channel_id=1, source_target_pairs={{0,16},{16,0},{1,17},{17,1},{2,18},{18,2},{3,19},{19,3},{4,20},{20... | collective-permute-start | bytes 3145736 | tf_op jit(solution)/shard_map/ppermute | solution.py:293

commit v2 on v1

--- a/solution.py
+++ b/solution.py
@@ -10,15 +10,16 @@
 
 
 def piece_width(depth):
-    for width in (768, 512, 256):
+    for width in (256,):
         if depth % (2 * width) == 0:
             return width
     return 128
 
 
 def kernel(
-    rows, pieces, x_ref, c_ref, o_ref, panel, same, other, acc,
-    p_recv, same_recv, other_recv, own_send, in_send, out_send,
+    rows, planes, pieces, x_ref, c_ref, direct_ref, outgoing_ref, panel, same, other, acc,
+    tile, flipped, tile_in, flipped_in,
+    p_recv, same_recv, other_recv, own_send, in_send, out_send, plane_recv, plane_send,
 ):
     half = pieces // 2
     mid = rows // 2
@@ -28,6 +29,8 @@
     core = b + 1 - 2 * (b % 2)
     beside = (b + 2) % 4
     opposite = 3 - b
+    plane = lax.axis_index("pw")
+    share = tile_in.shape[-2]
     side = z // mid
     m = z + side * (rows - 1 - 2 * z)
     step_in = 1 - 2 * side
@@ -43,14 +46,19 @@
     pl.semaphore_signal(barrier, inc=1, device_id={"col": beside}, device_id_type=MESH)
     pl.semaphore_signal(barrier, inc=1, device_id={"row": z_in}, device_id_type=MESH)
 
+    for distance in range(1, planes):
+        pl.semaphore_signal(
+            barrier, inc=1, device_id={"pw": (plane + distance) % planes}, device_id_type=MESH
+        )
+
     @pl.when(m > 0)
     def _():
         pl.semaphore_signal(barrier, inc=1, device_id={"row": z_out}, device_id_type=MESH)
-        pl.semaphore_wait(barrier, 4)
+        pl.semaphore_wait(barrier, 3 + planes)
 
     @pl.when(m == 0)
     def _():
-        pl.semaphore_wait(barrier, 3)
+        pl.semaphore_wait(barrier, 2 + planes)
 
     def copy(src, dst, send, recv, where):
         return pltpu.make_async_remote_copy(
@@ -64,10 +72,18 @@
     def order(i):
         return (i + half) % pieces
 
+    def span(q):
+        width = panel.shape[-1]
+        place = (q + side * half) % pieces
+        return pl.ds(pl.multiple_of(place * width, 128), width)
+
+    def own(q):
+        return x_ref.at[:, :, span(q)]
+
     def send_own(i):
         q = order(i)
-        copy(x_ref.at[q], panel.at[0, q], own_send.at[0, q], p_recv.at[0, q], {"col": core}).start()
-        copy(x_ref.at[q], panel.at[1, q], own_send.at[1, q], p_recv.at[1, q], {"col": beside}).start()
+        copy(own(q), panel.at[0, q], own_send.at[0, q], p_recv.at[0, q], {"col": core}).start()
+        copy(own(q), panel.at[1, q], own_send.at[1, q], p_recv.at[1, q], {"col": beside}).start()
 
     def send_inward(s):
         crossing = s < half * (m + 1)
@@ -79,7 +95,7 @@
 
         @pl.when(innermost & (back == 0))
         def _():
-            copy(x_ref.at[q], other.at[chunk, q], in_send.at[s], other_recv.at[chunk, q], where).start()
+            copy(own(q), other.at[chunk, q], in_send.at[s], other_recv.at[chunk, q], where).start()
 
         @pl.when(innermost & (back > 0))
         def _():
@@ -87,7 +103,7 @@
 
         @pl.when(jnp.logical_not(innermost) & (back == 0))
         def _():
-            copy(x_ref.at[q], same.at[chunk, q], in_send.at[s], same_recv.at[chunk, q], where).start()
+            copy(own(q), same.at[chunk, q], in_send.at[s], same_recv.at[chunk, q], where).start()
 
         if mid > 2:
             @pl.when(jnp.logical_not(innermost) & (back > 0))
@@ -100,16 +116,51 @@
         return m - 1 - rest // half, rest % half + jnp.where(crossing, 0, half)
 
     def multiply(chunk, q, target):
-        weighted = chunk[...] * c_ref[q]
+        weighted = chunk[...].reshape(acc.shape[2], -1) * c_ref[:, span(q)]
         high = weighted.astype(jnp.bfloat16)
         low = (weighted - high.astype(jnp.float32)).astype(jnp.bfloat16)
-        blocks = (x_ref.at[q], panel.at[0, q], panel.at[1, q], panel.at[2, q])
+        blocks = (own(q), panel.at[0, q], panel.at[1, q], panel.at[2, q])
         dims = (((1,), (1,)), ((), ()))
         for block, a in zip(blocks, (b, core, beside, opposite)):
-            left = block[...].astype(jnp.bfloat16)
+            left = block[...].reshape(acc.shape[2], -1).astype(jnp.bfloat16)
             acc[target, a] += lax.dot_general(
                 left, high, dims, preferred_element_type=jnp.float32
             ) + lax.dot_general(left, low, dims, preferred_element_type=jnp.float32)
+
+    def plane_copies(s, distance, kind):
+        target = (plane + distance) % planes
+        part = pl.ds(pl.multiple_of(target * share, share), share)
+        source, landing = ((tile, tile_in), (flipped, flipped_in))[kind]
+        return copy(
+            source.at[s, :, :, part, :], landing.at[distance - 1, s],
+            plane_send.at[kind, distance - 1, s], plane_recv.at[kind, distance - 1, s],
+            {"pw": target},
+        )
+
+    def finish(s):
+        def one(a, carry):
+            n = acc.shape[2] // 2
+            real = 2.0 * (acc[s, a, :n, :n] + acc[s, a, n:, n:])
+            imag = 2.0 * (acc[s, a, :n, n:] - acc[s, a, n:, :n])
+            tile[s, a, 0] = real
+            tile[s, a, 1] = imag
+            flipped[s, a, 0] = real.T
+            flipped[s, a, 1] = -imag.T
+            return carry
+
+        lax.fori_loop(0, 4, one, 0)
+        for distance in range(1, planes):
+            plane_copies(s, distance, 0).start()
+
+            @pl.when(s != z)
+            def _():
+                plane_copies(s, distance, 1).start()
+
+    def place_near(chunk):
+        return chunk + side * (rows - 1 - 2 * chunk)
+
+    def place_far(chunk):
+        return chunk + (1 - side) * (rows - 1 - 2 * chunk)
 
     for i in range(ahead):
         send_own(i)
@@ -165,41 +216,85 @@
         def _():
             q = order(t - 1)
             arrived(panel.at[2, q], p_recv.at[2, q])
-            multiply(x_ref.at[q], q, z)
+            multiply(own(q), q, z)
+
+            @pl.when(t == pieces)
+            def _():
+                finish(z)
 
         @pl.when((t >= half + 1) & (t - half - 1 < half * m))
         def _():
             chunk, q = outer_arrival(t - half - 1)
-            multiply(same.at[chunk, q], q, chunk + side * (rows - 1 - 2 * chunk))
+            multiply(same.at[chunk, q], q, place_near(chunk))
 
         @pl.when((t >= half * m) & (t < outer_count))
         def _():
             chunk, q = outer_arrival(t)
-            multiply(same.at[chunk, q], q, chunk + side * (rows - 1 - 2 * chunk))
+            multiply(same.at[chunk, q], q, place_near(chunk))
 
         w = t - 1 - lag
 
         @pl.when((w >= 0) & (w < cross_count))
         def _():
             chunk, q = mid - 1 - w // half, w % half
-            multiply(other.at[chunk, q], q + half, chunk + (1 - side) * (rows - 1 - 2 * chunk))
+            multiply(other.at[chunk, q], q + half, place_far(chunk))
+
+            @pl.when(q == half - 1)
+            def _():
+                finish(place_far(chunk))
 
         return carry
 
     steps = max(pieces + 1, cross_count + mid, 2 * half * (mid - 1))
     lax.fori_loop(0, steps, step, 0)
 
-    def finish(i, carry):
-        s, a = i // 4, i % 4
-        n = acc.shape[2] // 2
-        o_ref[s, a, 0] = 2.0 * (acc[s, a, :n, :n] + acc[s, a, n:, n:])
-        o_ref[s, a, 1] = 2.0 * (acc[s, a, :n, n:] - acc[s, a, n:, :n])
-        return carry
-
-    lax.fori_loop(0, rows * 4, finish, 0)
+    def finish_near(chunk, carry):
+        @pl.when(chunk < m)
+        def _():
+            finish(place_near(chunk))
+
+        return carry
+
+    lax.fori_loop(0, mid - 1, finish_near, 0)
+
+    def gather(s, carry):
+        far = s // mid != side
+        m_of = s + side * (rows - 1 - 2 * s)
+        mirrored = far | (m_of < m)
+        here = pl.ds(pl.multiple_of(plane * share, share), share)
+
+        @pl.when(mirrored | (s == z))
+        def _():
+            for distance in range(1, planes):
+                plane_copies(s, distance, 0).wait()
+            total = tile[s, :, :, here, :]
+            for distance in range(1, planes):
+                total += tile_in[distance - 1, s]
+            direct_ref[s] = total
+
+        @pl.when(mirrored)
+        def _():
+            for distance in range(1, planes):
+                plane_copies(s, distance, 1).wait()
+            total = flipped[s, :, :, here, :]
+            for distance in range(1, planes):
+                total += flipped_in[distance - 1, s]
+            outgoing_ref[s] = total
+
+        @pl.when(jnp.logical_not(mirrored))
+        def _():
+            outgoing_ref[s] = jnp.zeros(outgoing_ref.shape[1:], jnp.float32)
+
+        @pl.when(jnp.logical_not(mirrored | (s == z)))
+        def _():
+            direct_ref[s] = jnp.zeros(direct_ref.shape[1:], jnp.float32)
+
+        return carry
+
+    lax.fori_loop(0, rows, gather, 0)
 
     def left(send):
-        copy(x_ref.at[0], panel.at[0, 0], send, p_recv.at[0, 0], {"col": core}).wait_send()
+        copy(own(0), panel.at[0, 0], send, p_recv.at[0, 0], {"col": core}).wait_send()
 
     def drain_own(i, carry):
         left(own_send.at[0, i])
@@ -227,28 +322,38 @@
         lax.fori_loop(0, cross_count, drain_out, 0)
 
 
-def partial_tiles(x, c, row_count):
-    pieces, height, width = x.shape
+def summed_tiles(x, c, row_count, plane_count):
+    _, length, depth = x.shape
+    width = piece_width(depth)
+    pieces, height = depth // width, 2 * length
     half, mid = pieces // 2, row_count // 2
+    share = length // plane_count
+    result = jax.ShapeDtypeStruct((row_count, 4, 2, share, length), jnp.float32)
     return pl.pallas_call(
-        functools.partial(kernel, row_count, pieces),
-        out_shape=jax.ShapeDtypeStruct((row_count, 4, 2, height // 2, height // 2), jnp.float32),
+        functools.partial(kernel, row_count, plane_count, pieces),
+        out_shape=(result, result),
         in_specs=[pl.BlockSpec(memory_space=pltpu.VMEM)] * 2,
-        out_specs=pl.BlockSpec(memory_space=pltpu.VMEM),
+        out_specs=(pl.BlockSpec(memory_space=pltpu.VMEM),) * 2,
         scratch_shapes=[
-            pltpu.VMEM((3, pieces, height, width), jnp.float32),
-            pltpu.VMEM((max(mid - 1, 1), pieces, height, width), jnp.float32),
-            pltpu.VMEM((mid, half, height, width), jnp.float32),
+            pltpu.VMEM((3, pieces, 2, length, width), jnp.float32),
+            pltpu.VMEM((max(mid - 1, 1), pieces, 2, length, width), jnp.float32),
+            pltpu.VMEM((mid, half, 2, length, width), jnp.float32),
             pltpu.VMEM((row_count, 4, height, height), jnp.float32),
+            pltpu.VMEM((row_count, 4, 2, length, length), jnp.float32),
+            pltpu.VMEM((row_count, 4, 2, length, length), jnp.float32),
+            pltpu.VMEM((plane_count - 1, row_count, 4, 2, share, length), jnp.float32),
+            pltpu.VMEM((plane_count - 1, row_count, 4, 2, share, length), jnp.float32),
             pltpu.SemaphoreType.DMA((3, pieces)),
             pltpu.SemaphoreType.DMA((max(mid - 1, 1), pieces)),
             pltpu.SemaphoreType.DMA((mid, half)),
             pltpu.SemaphoreType.DMA((3, pieces)),
             pltpu.SemaphoreType.DMA((2 * half * mid,)),
             pltpu.SemaphoreType.DMA((half * mid,)),
+            pltpu.SemaphoreType.DMA((2, plane_count - 1, row_count)),
+            pltpu.SemaphoreType.DMA((2, plane_count - 1, row_count)),
         ],
         compiler_params=pltpu.CompilerParams(
-            collective_id=0, has_side_effects=True, vmem_limit_bytes=56 * 2**20
+            collective_id=0, has_side_effects=True, vmem_limit_bytes=58 * 2**20
         ),
     )(x, c)
 
@@ -256,7 +361,7 @@
 def per_device(
     pair_density, coulomb, valence_band, conduction_band, valence_energy, conduction_energy
 ):
-    tile_len, _, depth = pair_density.shape
+    tile_len = pair_density.shape[0]
     row_count = lax.axis_size("row")
     col_count = lax.axis_size("col")
     plane_count = lax.axis_size("pw")
@@ -266,36 +371,14 @@
     plane_here = lax.axis_index("pw")
     assert col_count == 4 and row_count % 2 == 0
 
-    width = piece_width(depth)
-    pieces = depth // width
-    far_side = row_here >= row_count // 2
-
-    def from_side(array):
-        return jnp.where(far_side, jnp.roll(array, pieces // 2, axis=0), array)
-
-    x = jnp.transpose(pair_density.reshape(tile_len, 2, pieces, width), (2, 1, 0, 3))
-    x = from_side(x.reshape(pieces, 2 * tile_len, width)).astype(jnp.float32)
-    c = from_side(coulomb.reshape(pieces, 1, width))
-    blocks = partial_tiles(x, c, row_count)
-
-    def shares(plane):
-        rows = lax.dynamic_slice_in_dim(blocks, plane * share_len, share_len, 3)
-        cols = lax.dynamic_slice_in_dim(blocks, plane * share_len, share_len, 4)
-        rows = jnp.transpose(rows, (1, 3, 2, 0, 4))
-        cols = jnp.transpose(cols, (0, 1, 2, 4, 3))
-        return rows, cols
-
-    direct, outgoing = shares(plane_here)
-    for distance in range(1, plane_count):
-        route = [(i, (i + distance) % plane_count) for i in range(plane_count)]
-        rows, cols = shares(jnp.remainder(plane_here + distance, plane_count))
-        outgoing = outgoing + lax.ppermute(cols, "pw", route)
-        direct = direct + lax.ppermute(rows, "pw", route)
+    x = jnp.stack([pair_density[:, 0, :], pair_density[:, 1, :]]).astype(jnp.float32)
+    c = coulomb[None, :]
+    direct, outgoing = summed_tiles(x, c, row_count, plane_count)
+    direct = jnp.transpose(direct, (1, 3, 2, 0, 4))
     outgoing = outgoing.reshape(row_count * col_count, 2, share_len, tile_len)
     incoming = lax.all_to_all(outgoing, ("row", "col"), split_axis=0, concat_axis=0, tiled=True)
     incoming = incoming.reshape(row_count, col_count, 2, share_len, tile_len)
-    conjugate = jnp.array([1.0, -1.0], jnp.float32)
-    mirrored = jnp.transpose(incoming, (1, 3, 2, 0, 4)) * conjugate[None, None, :, None, None]
+    mirrored = jnp.transpose(incoming, (1, 3, 2, 0, 4))
     elsewhere = (jnp.arange(row_count, dtype=jnp.int32) != row_here)[None, None, None, :, None]
     reduced = direct + jnp.where(elsewhere, mirrored, 0.0)
     own_valence = lax.dynamic_slice_in_dim(valence_band, plane_here * share_len, share_len, 0)

time: 258 us -> 225 us (0.87)
  Pallas kernels: 158 us -> 178 us
  waiting for transfers between devices: 44.1 us -> 24.1 us
  local copies, waits for them, and re-layouts: 25.2 us -> 11.6 us
  starting transfers between devices: 17 us -> 5.93 us
  other arithmetic: 11.4 us -> 5.23 us
    ppermute x2 -> x0, waiting for transfers between devices: 44.1 us -> none  [the longest x1 22.7 us: per_device(): direct = direct + lax.ppermute(rows, 'pw', route)]
    all_to_all x1, waiting for transfers between devices: 0.01 us -> 24.1 us  [per_device(): lax.all_to_all(outgoing, ('row', 'col'), split_axis=0, concat_axis=0, til...]
    pallas_call x1, Pallas kernels: 158 us -> 178 us  [summed_tiles(): pl.pallas_call(functools.partial(kernel, row_count, plane_count, pieces),...]
    reshape x3 -> x0, local copies, waits for them, and re-layouts: 14.1 us -> none  [the longest x2 10.9 us: per_device(): pair_density.reshape(tile_len, 2, pieces, width)]
    all_to_all x1, starting transfers between devices: 14.4 us -> 5.93 us  [per_device(): lax.all_to_all(outgoing, ('row', 'col'), split_axis=0, concat_axis=0, til...]
    slice x2 -> x1, local copies, waits for them, and re-layouts: 1.92 us -> 7.59 us  [per_device(): pair_density[:, 0, :]]
    transpose x3 -> x0, local copies, waits for them, and re-layouts: 3.83 us -> none  [the longest x2 2.79 us: shares(): cols = jnp.transpose(cols, (0, 1, 2, 4, 3))]
    add x1 -> x0, other arithmetic: 3.54 us -> none  [per_device(): outgoing = outgoing + lax.ppermute(cols, 'pw', route)]
  transfers between devices with their start and end apart: 3 -> 1, of which waited for: 2 -> 1; matrix products, arithmetic and copies ran while one was open for 1% -> 0% of each run, Pallas kernels for 0% -> 0%
where the time goes in v2:
time: 225 us
  Pallas kernels  178 us (79%)
  waiting for transfers between devices  24.1 us (11%)
  local copies, waits for them, and re-layouts  11.6 us (5%)
  starting transfers between devices  5.93 us (3%)
  other arithmetic  5.23 us (2%)
    pallas_call x1, Pallas kernels, summed_tiles(): pl.pallas_call(functools.partial(kernel, row_count, plane_count, pieces),...  178 us
    all_to_all x1, waiting for transfers between devices, per_device(): lax.all_to_all(outgoing, ('row', 'col'), split_axis=0, concat_axis=0, til...  24.1 us
    slice x1, local copies, waits for them, and re-layouts, per_device(): pair_density[:, 0, :]  7.59 us
    all_to_all x1, starting transfers between devices, per_device(): lax.all_to_all(outgoing, ('row', 'col'), split_axis=0, concat_axis=0, til...  5.93 us
  transfers between devices with their start and end apart: 1, of which 1 were waited for; matrix products, arithmetic and copies ran while one was open for 0% of the time, Pallas kernels for 0%

profile of v2, /device:TPU:11, one launch (start us, length us, event | category | flops | bytes accessed | tf_op | source)
XLA Modules:
  0.0 224.9 jit_solution(14878829867586052791)
XLA Ops:
  0.0 7.6 %fusion.1 = (bf16[128,1,6144]{2,1,0:T(2,128)(2,1)S(1)}, bf16[128,1,6144]{2,1,0:T(2,128)(2,1)S(1)}) fusion(bf16[128,2,6144]{2,1,0:T(2,128)(2,1)} %param.6), kind=kLoop, calls=%fused_computation.17 | loop fusion | bytes 6291456 | tf_op jit(solution)/shard_map/slice | solution.py:374
  7.6 1.8 copy_bitcast_fusion
  9.4 3.1 %maximum_convert_fusion.x_ref = f32[2,128,6144]{2,1,0:T(8,128)} fusion(bf16[1,128,6144]{2,1,0:T(8,128)(2,1)S(1)} %get-tuple-element.11, bf16[1,128,6144]{2,1,0:T(8,128)(2,1)S(1)} %get-tuple-element.12), kind=kLoop, calls=%fused_computation | loop fusion | flops 3145728 | bytes 9437184 | tf_op jit(solution)/shard_map/convert_element_type | solution.py:374
  12.5 0.0 copy-start.1
  12.5 0.0 copy-start.2
  12.5 0.0 copy-start.3
  12.5 0.0 copy-start
  12.5 178.0 %shard_map.64 = (f32[4,4,2,64,128]{4,3,2,1,0:T(8,128)}, f32[4,4,2,64,128]{4,3,2,1,0:T(8,128)}) custom-call(f32[2,128,6144]{2,1,0:T(8,128)} %maximum_convert_fusion.x_ref, f32[1,6144]{1,0:T(1,128)} %bitcast.15), custom_call_target="tpu_custom_call" | custom-call | tf_op jit(solution)/shard_map/pallas_call | solution.py:332
  190.4 5.9 %all-to-all-start = ((f32[16,2,64,128]{3,2,1,0:T(8,128)}), f32[16,2,64,128]{3,2,1,0:T(8,128)S(1)}, u32[]{:S(2)}, u32[]{:S(2)}) async-start(f32[16,2,64,128]{3,2,1,0:T(8,128)} %bitcast.14), calls=%async_computation | async-start | bytes 2097152 | tf_op jit(solution)/shard_map/all_to_all | solution.py:379
  196.4 0.0 copy-done.1
  196.4 0.1 dynamic_slice.6
  196.4 0.0 copy-done.2
  196.4 0.1 dynamic_slice.7
  196.5 0.0 copy-done.3
  196.5 0.1 select_reduce_fusion.1
  196.6 0.0 copy-done
  196.6 0.2 select_reduce_fusion
  196.9 0.1 broadcast_and_fusion.1
  196.9 0.1 broadcast_and_fusion
  197.0 0.1 iota_compare_fusion.1
  197.1 24.1 %all-to-all-done = f32[16,2,64,128]{3,2,1,0:T(8,128)S(1)} async-done(((f32[16,2,64,128]{3,2,1,0:T(8,128)}), f32[16,2,64,128]{3,2,1,0:T(8,128)S(1)}, u32[]{:S(2)}, u32[]{:S(2)}) %all-to-all-start) | async-done | bytes 1048608 | tf_op jit(solution)/shard_map/all_to_all | solution.py:379
  221.2 1.6 fusion
  222.9 2.1 copy.12
  (5 shorter events, 0.0 us)
Async XLA Ops:
  12.5 183.9 %copy-start.1 = (s32[128]{0:T(128)S(1)}, s32[128]{0:T(128)}, u32[]{:S(2)}) copy-start(s32[128]{0:T(128)} %param.9) | copy-start | bytes 1540
  12.5 184.0 %copy-start.2 = (s32[128]{0:T(128)S(1)}, s32[128]{0:T(128)}, u32[]{:S(2)}) copy-start(s32[128]{0:T(128)} %param.8) | copy-start | bytes 1540
  12.5 184.1 %copy-start.3 = (f32[32]{0:T(128)S(1)}, f32[32]{0:T(128)}, u32[]{:S(2)}) copy-start(f32[32]{0:T(128)} %param.11) | copy-start | bytes 388
  12.5 184.2 %copy-start = (f32[512]{0:T(512)S(1)}, f32[512]{0:T(512)}, u32[]{:S(2)}) copy-start(f32[512]{0:T(512)} %param.10) | copy-start | bytes 6148
  190.4 30.8 %all-to-all-start = ((f32[16,2,64,128]{3,2,1,0:T(8,128)}), f32[16,2,64,128]{3,2,1,0:T(8,128)S(1)}, u32[]{:S(2)}, u32[]{:S(2)}) async-start(f32[16,2,64,128]{3,2,1,0:T(8,128)} %bitcast.14), calls=%async_computation | async-start | bytes 2097152 | tf_op jit(solution)/shard_map/all_to_all | solution.py:379

commit v3 on v2

--- a/solution.py
+++ b/solution.py
@@ -17,9 +17,10 @@
 
 
 def kernel(
-    rows, planes, pieces, x_ref, c_ref, direct_ref, outgoing_ref, panel, same, other, acc,
-    tile, flipped, tile_in, flipped_in,
+    rows, planes, pieces, x_ref, c_ref, o_ref, panel, same, other, acc,
+    tile, flipped, tile_in, flipped_in, outgoing, incoming,
     p_recv, same_recv, other_recv, own_send, in_send, out_send, plane_recv, plane_send,
+    mirror_recv, mirror_send,
 ):
     half = pieces // 2
     mid = rows // 2
@@ -42,23 +43,20 @@
     inner_sends = jnp.where(innermost, half * (m + 1), 2 * half * (m + 1))
 
     barrier = pltpu.get_barrier_semaphore()
-    pl.semaphore_signal(barrier, inc=1, device_id={"col": core}, device_id_type=MESH)
-    pl.semaphore_signal(barrier, inc=1, device_id={"col": beside}, device_id_type=MESH)
-    pl.semaphore_signal(barrier, inc=1, device_id={"row": z_in}, device_id_type=MESH)
-
+    def greet(i, carry):
+        other_one = (z * 4 + b + i) % (rows * 4)
+        pl.semaphore_signal(
+            barrier, inc=1, device_id={"row": other_one // 4, "col": other_one % 4},
+            device_id_type=MESH,
+        )
+        return carry
+
+    lax.fori_loop(1, rows * 4, greet, 0)
     for distance in range(1, planes):
         pl.semaphore_signal(
             barrier, inc=1, device_id={"pw": (plane + distance) % planes}, device_id_type=MESH
         )
-
-    @pl.when(m > 0)
-    def _():
-        pl.semaphore_signal(barrier, inc=1, device_id={"row": z_out}, device_id_type=MESH)
-        pl.semaphore_wait(barrier, 3 + planes)
-
-    @pl.when(m == 0)
-    def _():
-        pl.semaphore_wait(barrier, 2 + planes)
+    pl.semaphore_wait(barrier, rows * 4 + planes - 2)
 
     def copy(src, dst, send, recv, where):
         return pltpu.make_async_remote_copy(
@@ -149,12 +147,15 @@
             return carry
 
         lax.fori_loop(0, 4, one, 0)
+
+        @pl.when(s != z)
+        def _():
+            for distance in range(1, planes):
+                plane_copies(s, distance, 1).start()
+
+    def send_direct(s):
         for distance in range(1, planes):
             plane_copies(s, distance, 0).start()
-
-            @pl.when(s != z)
-            def _():
-                plane_copies(s, distance, 1).start()
 
     def place_near(chunk):
         return chunk + side * (rows - 1 - 2 * chunk)
@@ -243,6 +244,10 @@
             def _():
                 finish(place_far(chunk))
 
+                @pl.when(chunk > 0)
+                def _():
+                    send_direct(place_far(chunk))
+
         return carry
 
     steps = max(pieces + 1, cross_count + mid, 2 * half * (mid - 1))
@@ -256,42 +261,103 @@
         return carry
 
     lax.fori_loop(0, mid - 1, finish_near, 0)
+
+    send_direct(place_far(0))
+    send_direct(z)
+
+    def direct_near(chunk, carry):
+        @pl.when(chunk < m)
+        def _():
+            send_direct(place_near(chunk))
+
+        return carry
+
+    lax.fori_loop(0, mid - 1, direct_near, 0)
+    here = pl.ds(pl.multiple_of(plane * share, share), share)
+
+    def mirror_copy(s, a):
+        return copy(
+            outgoing.at[s, a], incoming.at[z, b], mirror_send.at[s, a], mirror_recv.at[z, b],
+            {"row": s, "col": a},
+        )
+
+    def send_mirrored(s):
+        for distance in range(1, planes):
+            plane_copies(s, distance, 1).wait()
+        total = flipped[s, :, :, here, :]
+        for distance in range(1, planes):
+            total += flipped_in[distance - 1, s]
+        outgoing[s] = total
+
+        def one(a, carry):
+            mirror_copy(s, a).start()
+            return carry
+
+        lax.fori_loop(0, 4, one, 0)
+
+    def mirror_far(i, carry):
+        send_mirrored(place_far(mid - 1 - i))
+        return carry
+
+    lax.fori_loop(0, mid, mirror_far, 0)
+
+    def mirror_near(chunk, carry):
+        @pl.when(chunk < m)
+        def _():
+            send_mirrored(place_near(chunk))
+
+        return carry
+
+    lax.fori_loop(0, mid - 1, mirror_near, 0)
 
     def gather(s, carry):
         far = s // mid != side
         m_of = s + side * (rows - 1 - 2 * s)
-        mirrored = far | (m_of < m)
-        here = pl.ds(pl.multiple_of(plane * share, share), share)
-
-        @pl.when(mirrored | (s == z))
+        computed = far | (m_of <= m)
+
+        @pl.when(computed)
         def _():
             for distance in range(1, planes):
                 plane_copies(s, distance, 0).wait()
             total = tile[s, :, :, here, :]
             for distance in range(1, planes):
                 total += tile_in[distance - 1, s]
-            direct_ref[s] = total
-
-        @pl.when(mirrored)
-        def _():
-            for distance in range(1, planes):
-                plane_copies(s, distance, 1).wait()
-            total = flipped[s, :, :, here, :]
-            for distance in range(1, planes):
-                total += flipped_in[distance - 1, s]
-            outgoing_ref[s] = total
-
-        @pl.when(jnp.logical_not(mirrored))
-        def _():
-            outgoing_ref[s] = jnp.zeros(outgoing_ref.shape[1:], jnp.float32)
-
-        @pl.when(jnp.logical_not(mirrored | (s == z)))
-        def _():
-            direct_ref[s] = jnp.zeros(direct_ref.shape[1:], jnp.float32)
+            o_ref[s] = total
+
+        @pl.when(jnp.logical_not(computed))
+        def _():
+            o_ref[s] = jnp.zeros(o_ref.shape[1:], jnp.float32)
 
         return carry
 
     lax.fori_loop(0, rows, gather, 0)
+
+    def receive(i, carry):
+        s, a = i // 4, i % 4
+        far = s // mid != side
+        m_of = s + side * (rows - 1 - 2 * s)
+
+        @pl.when(far | (m_of > m))
+        def _():
+            arrived(incoming.at[s, a], mirror_recv.at[s, a])
+            o_ref[s, a] += incoming[s, a]
+
+        return carry
+
+    lax.fori_loop(0, rows * 4, receive, 0)
+
+    def drain_mirror(i, carry):
+        s, a = i // 4, i % 4
+        far = s // mid != side
+        m_of = s + side * (rows - 1 - 2 * s)
+
+        @pl.when(far | (m_of < m))
+        def _():
+            mirror_copy(s, a).wait_send()
+
+        return carry
+
+    lax.fori_loop(0, rows * 4, drain_mirror, 0)
 
     def left(send):
         copy(own(0), panel.at[0, 0], send, p_recv.at[0, 0], {"col": core}).wait_send()
@@ -331,9 +397,9 @@
     result = jax.ShapeDtypeStruct((row_count, 4, 2, share, length), jnp.float32)
     return pl.pallas_call(
         functools.partial(kernel, row_count, plane_count, pieces),
-        out_shape=(result, result),
+        out_shape=result,
         in_specs=[pl.BlockSpec(memory_space=pltpu.VMEM)] * 2,
-        out_specs=(pl.BlockSpec(memory_space=pltpu.VMEM),) * 2,
+        out_specs=pl.BlockSpec(memory_space=pltpu.VMEM),
         scratch_shapes=[
             pltpu.VMEM((3, pieces, 2, length, width), jnp.float32),
             pltpu.VMEM((max(mid - 1, 1), pieces, 2, length, width), jnp.float32),
@@ -343,6 +409,8 @@
             pltpu.VMEM((row_count, 4, 2, length, length), jnp.float32),
             pltpu.VMEM((plane_count - 1, row_count, 4, 2, share, length), jnp.float32),
             pltpu.VMEM((plane_count - 1, row_count, 4, 2, share, length), jnp.float32),
+            pltpu.VMEM((row_count, 4, 2, share, length), jnp.float32),
+            pltpu.VMEM((row_count, 4, 2, share, length), jnp.float32),
             pltpu.SemaphoreType.DMA((3, pieces)),
             pltpu.SemaphoreType.DMA((max(mid - 1, 1), pieces)),
             pltpu.SemaphoreType.DMA((mid, half)),
@@ -351,6 +419,8 @@
             pltpu.SemaphoreType.DMA((half * mid,)),
             pltpu.SemaphoreType.DMA((2, plane_count - 1, row_count)),
             pltpu.SemaphoreType.DMA((2, plane_count - 1, row_count)),
+            pltpu.SemaphoreType.DMA((row_count, 4)),
+            pltpu.SemaphoreType.DMA((row_count, 4)),
         ],
         compiler_params=pltpu.CompilerParams(
             collective_id=0, has_side_effects=True, vmem_limit_bytes=58 * 2**20
@@ -373,14 +443,7 @@
 
     x = jnp.stack([pair_density[:, 0, :], pair_density[:, 1, :]]).astype(jnp.float32)
     c = coulomb[None, :]
-    direct, outgoing = summed_tiles(x, c, row_count, plane_count)
-    direct = jnp.transpose(direct, (1, 3, 2, 0, 4))
-    outgoing = outgoing.reshape(row_count * col_count, 2, share_len, tile_len)
-    incoming = lax.all_to_all(outgoing, ("row", "col"), split_axis=0, concat_axis=0, tiled=True)
-    incoming = incoming.reshape(row_count, col_count, 2, share_len, tile_len)
-    mirrored = jnp.transpose(incoming, (1, 3, 2, 0, 4))
-    elsewhere = (jnp.arange(row_count, dtype=jnp.int32) != row_here)[None, None, None, :, None]
-    reduced = direct + jnp.where(elsewhere, mirrored, 0.0)
+    reduced = jnp.transpose(summed_tiles(x, c, row_count, plane_count), (1, 3, 2, 0, 4))
     own_valence = lax.dynamic_slice_in_dim(valence_band, plane_here * share_len, share_len, 0)
     own_conduction = lax.dynamic_slice_in_dim(conduction_band, plane_here * share_len, share_len, 0)
     valence_ids = jnp.arange(valence_energy.shape[0], dtype=jnp.int32)

time: 225 us -> 201 us (0.89)
  waiting for transfers between devices: 24.1 us -> 0 us
  starting transfers between devices: 5.93 us -> 0 us
  Pallas kernels: 178 us -> 182 us
    all_to_all x1 -> x0, waiting for transfers between devices: 24.1 us -> none  [per_device(): lax.all_to_all(outgoing, ('row', 'col'), split_axis=0, concat_axis=0, til...]
    all_to_all x1 -> x0, starting transfers between devices: 5.93 us -> none  [per_device(): lax.all_to_all(outgoing, ('row', 'col'), split_axis=0, concat_axis=0, til...]
    pallas_call x1, Pallas kernels: 178 us -> 182 us  [summed_tiles(): pl.pallas_call(functools.partial(kernel, row_count, plane_count, pieces),...]
  transfers between devices with their start and end apart: 1 -> 0, of which waited for: 1 -> 0; matrix products, arithmetic and copies ran while one was open for 0% -> 0% of each run, Pallas kernels for 0% -> 0%
where the time goes in v3:
time: 201 us; the launch traced here: 199 us
  Pallas kernels  182 us (91%)
  local copies, waits for them, and re-layouts  11.5 us (6%)
  other arithmetic  5.1 us (3%)
    pallas_call x1, Pallas kernels, summed_tiles(): pl.pallas_call(functools.partial(kernel, row_count, plane_count, pieces),...  182 us
    slice x1, local copies, waits for them, and re-layouts, per_device(): pair_density[:, 0, :]  7.49 us

profile of v3, /device:TPU:11, one launch (start us, length us, event | category | flops | bytes accessed | tf_op | source)
XLA Modules:
  0.0 198.9 jit_solution(10949034976232160854)
XLA Ops:
  0.0 7.5 %fusion.1 = (bf16[128,1,6144]{2,1,0:T(2,128)(2,1)S(1)}, bf16[128,1,6144]{2,1,0:T(2,128)(2,1)S(1)}) fusion(bf16[128,2,6144]{2,1,0:T(2,128)(2,1)} %param.6), kind=kLoop, calls=%fused_computation.16 | loop fusion | bytes 6291456 | tf_op jit(solution)/shard_map/slice | solution.py:444
  7.5 1.8 copy_bitcast_fusion
  9.3 3.1 %maximum_convert_fusion.x_ref = f32[2,128,6144]{2,1,0:T(8,128)} fusion(bf16[1,128,6144]{2,1,0:T(8,128)(2,1)S(1)} %get-tuple-element.7, bf16[1,128,6144]{2,1,0:T(8,128)(2,1)S(1)} %get-tuple-element.8), kind=kLoop, calls=%fused_computation | loop fusion | flops 3145728 | bytes 9437184 | tf_op jit(solution)/shard_map/convert_element_type | solution.py:444
  12.3 0.0 copy-start.1
  12.4 0.0 copy-start.2
  12.4 0.0 copy-start.3
  12.4 0.0 copy-start
  12.4 182.2 %shard_map.64 = f32[4,4,2,64,128]{4,3,2,1,0:T(8,128)} custom-call(f32[2,128,6144]{2,1,0:T(8,128)} %maximum_convert_fusion.x_ref, f32[1,6144]{1,0:T(1,128)} %bitcast.11), custom_call_target="tpu_custom_call" | custom-call | tf_op jit(solution)/shard_map/pallas_call | solution.py:398
  194.6 0.0 copy-done.1
  194.6 0.1 dynamic_slice.6
  194.7 0.0 copy-done.2
  194.7 0.1 select_reduce_fusion.1
  194.7 0.0 copy-done.3
  194.8 0.1 dynamic_slice.7
  194.8 0.0 copy-done
  194.8 0.2 select_reduce_fusion
  195.0 0.1 iota_compare_fusion.1
  195.1 0.1 broadcast_and_fusion.1
  195.2 0.1 broadcast_and_fusion
  195.3 1.5 fusion
  196.8 2.1 %copy.12 = f32[1,4,64,2,4,1,128]{6,5,4,3,2,1,0:T(1,128)} copy(f32[1,4,64,2,4,1,128]{6,2,3,1,4,5,0:T(8,128)S(1)} %fusion) | data formatting | bytes 2097152 | tf_op jit(solution)/shard_map/reshape | solution.py:472
  (4 shorter events, 0.0 us)
Async XLA Ops:
  12.3 182.2 %copy-start.1 = (s32[128]{0:T(128)S(1)}, s32[128]{0:T(128)}, u32[]{:S(2)}) copy-start(s32[128]{0:T(128)} %param.9) | copy-start | bytes 1540
  12.4 182.3 %copy-start.2 = (f32[32]{0:T(128)S(1)}, f32[32]{0:T(128)}, u32[]{:S(2)}) copy-start(f32[32]{0:T(128)} %param.11) | copy-start | bytes 388
  12.4 182.4 %copy-start.3 = (s32[128]{0:T(128)S(1)}, s32[128]{0:T(128)}, u32[]{:S(2)}) copy-start(s32[128]{0:T(128)} %param.8) | copy-start | bytes 1540
  12.4 182.5 %copy-start = (f32[512]{0:T(512)S(1)}, f32[512]{0:T(512)}, u32[]{:S(2)}) copy-start(f32[512]{0:T(512)} %param.10) | copy-start | bytes 6148
